TPU v7x, 32 devices: a whole 2x2x4 slice. The times are simulated.
32 devices in a mesh: dp: 16 (over z, y, core), seq: 2 (over x).
Axes of the slice: x: 2, y: 2, z: 4, core: 2. Of those that a mesh axis runs over, the one named last changes fastest.
Arguments:
- short_tokens: bfloat16 [128, 128, 768], P(('dp', 'seq')), may hold values from -6 to 6
- long_tokens: bfloat16 [32, 512, 768], P('dp', 'seq'), may hold values from -6 to 6
- short_len: int32 [128], P(('dp', 'seq')), may hold values from 1 to 128, as said below
- long_len: int32 [32], P('dp'), may hold values from 129 to 512, as said below
- short_pool: int32 [128, 128], P(('dp', 'seq')), may hold values 0 or 1
- long_pool: int32 [32, 512], P('dp', 'seq'), may hold values 0 or 1
- short_cot: bfloat16 [128, 128, 768], P(('dp', 'seq')), may hold values from -6 to 6
- long_cot: bfloat16 [32, 512, 768], P('dp', 'seq'), may hold values from -6 to 6
- short_pool_cot: float32 [128, 768], P(('dp', 'seq')), may hold values from -6 to 6
- long_pool_cot: float32 [32, 768], P('dp'), may hold values from -6 to 6
- w_qkv: bfloat16 [768, 2304], P(('dp', 'seq')), may hold values from -0.21875 to 0.21875
- w_out: bfloat16 [768, 768], P(('dp', 'seq')), may hold values from -0.625 to 0.625
- w_up: bfloat16 [768, 3072], P(('dp', 'seq')), may hold values from -0.21875 to 0.21875
- w_down: bfloat16 [3072, 768], P(('dp', 'seq')), may hold values from -0.109375 to 0.109375
- qv_bias: bfloat16 [768, 2], P(('dp', 'seq')), may hold values from -3 to 3
- out_bias: bfloat16 [768, 2], P(('dp', 'seq')), may hold values from -3 to 3
- up_bias: bfloat16 [3072], P(('dp', 'seq')), may hold values from -3 to 3
- norm_gain: bfloat16 [768, 2], P(('dp', 'seq')), may hold values from 0.25 to 1.75
- norm_shift: bfloat16 [768, 2], P(('dp', 'seq')), may hold values from -3 to 3
Outputs:
- short_out: bfloat16 [128, 128, 768], P(('dp', 'seq'))
- long_out: bfloat16 [32, 512, 768], P('dp', 'seq')
- short_pooled: float32 [128, 768], P(('dp', 'seq'))
- long_pooled: float32 [32, 768], P('dp')
- short_grad_in: float32 [128, 128, 768], P(('dp', 'seq'))
- long_grad_in: float32 [32, 512, 768], P('dp', 'seq')
- grad_w_qkv: float32 [768, 2304], P(('dp', 'seq'))
- grad_w_out: float32 [768, 768], P(('dp', 'seq'))
- grad_w_up: float32 [768, 3072], P(('dp', 'seq'))
- grad_w_down: float32 [3072, 768], P(('dp', 'seq'))
- grad_qv_bias: float32 [768, 2], P(('dp', 'seq'))
- grad_out_bias: float32 [768, 2], P(('dp', 'seq'))
- grad_up_bias: float32 [3072], P(('dp', 'seq'))
- grad_norm_gain: float32 [768, 2], P(('dp', 'seq'))
- grad_norm_shift: float32 [768, 2], P(('dp', 'seq'))
Inputs may be any that keep to these rules, and one draw needn't show every extreme that they name: `short_len`: among the 4 short sequences of each device, one has length exactly 128. `long_len`: among the 2 passages of each dp index, one has length exactly 512.
All inputs are finite; a program needn't handle non-finite values. No bound on the sum of `short_pool` or of `long_pool` on one device may be relied on, other than what follows from the above.
Results may differ from a plain program's by a relative error of at most 0.013.
Values may be sent and summed in bfloat16 or wider, within the bound.
A program may use at most 256 MiB of HBM per device.

v0:
```python
import functools
import math

import jax
import jax.numpy as jnp
from jax import lax
from jax.experimental import pallas as pl
from jax.experimental.pallas import tpu as pltpu
from jax.sharding import PartitionSpec as P

HEADS = 12
EPS = 1e-12
MESH = pl.DeviceIdType.MESH

SIZES = (80, 32, 96, 96)
GATHER_X = (48, 16, 48, 48)
SUMS = (80, 80, 80, 32, 96, 96)
SUMS_X = (48, 48, 32, 16, 48, 48)


FLIPS = ((0, 0), (0, 1), (1, 0), (1, 1))


class Place:
    def __init__(self):
        dp = lax.axis_index("dp")
        self.x = lax.axis_index("seq")
        self.groups = lax.axis_size("dp") // 4
        self.z = lax.div(dp, 4)
        self.y = lax.rem(lax.div(dp, 2), 2)
        self.c = lax.rem(dp, 2)
        self.dp = dp

    def z_of(self, step):
        if step == 1:
            return self.z + 1 - 2 * lax.rem(self.z, 2)
        return lax.rem(self.z + 2, 4) if step == 2 else 3 - self.z

    def at_z(self, step):
        return (self.z_of(step) * 4 + self.y * 2 + self.c, self.x)

    def at_x(self):
        return (self.dp, 1 - self.x)

    def at_y(self):
        return (self.z * 4 + (1 - self.y) * 2 + self.c, self.x)

    def at_core(self):
        return (self.z * 4 + self.y * 2 + 1 - self.c, self.x)

    def slot(self, flip_y=0, flip_c=0, flip_x=0):
        y = 1 - self.y if flip_y else self.y
        c = 1 - self.c if flip_c else self.c
        x = 1 - self.x if flip_x else self.x
        return y * 4 + c * 2 + x

    def z_back(self, step):
        return self.z if step == 0 else self.z_of(step)

    def partners(self):
        return [self.at_z(step) for step in range(1, self.groups)] + [
            self.at_x(),
            self.at_y(),
            self.at_core(),
        ]

    def greet_start(self):
        for partner in self.partners():
            pl.semaphore_signal(
                pltpu.get_barrier_semaphore(), inc=1, device_id=partner, device_id_type=MESH
            )

    def greet_wait(self):
        pl.semaphore_wait(pltpu.get_barrier_semaphore(), len(self.partners()))


class Wires:
    def __init__(self, send, recv):
        self.send, self.recv, self.sent, self.left = send, recv, [], set()

    def put(self, src, dst, to):
        number = len(self.sent)
        copy = pltpu.make_async_remote_copy(
            src_ref=src,
            dst_ref=dst,
            send_sem=self.send.at[number],
            recv_sem=self.recv.at[number],
            device_id=to,
            device_id_type=MESH,
        )
        copy.start()
        self.sent.append(copy)
        return (number, to)

    def landed(self, ticket, ref):
        number, to = ticket
        pltpu.make_async_remote_copy(
            src_ref=ref,
            dst_ref=ref,
            send_sem=self.send.at[number],
            recv_sem=self.recv.at[number],
            device_id=to,
            device_id_type=MESH,
        ).wait_recv()

    def has_left(self, ticket):
        self.sent[ticket[0]].wait_send()
        self.left.add(ticket[0])

    def close(self):
        for number, copy in enumerate(self.sent):
            if number not in self.left:
                copy.wait_send()


class Gather:
    def __init__(self, wires, place, wholes, last):
        self.wires, self.place, self.wholes, self.last = wires, place, wholes, last
        self.steps = place.groups
        self.along_z, self.along_x, self.along_y = {}, {}, {}
        self.by_x, self.by_y, self.core = {}, {}, {}

    def halves(self, k):
        some = GATHER_X[k]
        return pl.ds(0, some), pl.ds(some, SIZES[k] - some)

    def start(self, k):
        place, wires = self.place, self.wires
        dst = self.wholes[k].at[place.z, place.slot()]
        src = self.last if k == 3 else dst
        for step in range(1, self.steps):
            self.along_z[k, step] = wires.put(src, dst, place.at_z(step))

    def start_plane(self, k):
        place, wires = self.place, self.wires
        dst = self.wholes[k].at[place.z, place.slot()]
        src = self.last if k == 3 else dst
        self.along_x[k, 0] = wires.put(src, dst, place.at_x())
        self.along_y[k, 0] = wires.put(src, dst, place.at_y())
        self.core[k, 0, 0] = wires.put(src, dst, place.at_core())

    def relay_z(self, k):
        place, wires = self.place, self.wires
        for step in range(1, self.steps):
            ref = self.wholes[k].at[place.z_back(step), place.slot()]
            wires.landed(self.along_z[k, step], ref)
            self.along_x[k, step] = wires.put(ref, ref, place.at_x())
            self.along_y[k, step] = wires.put(ref, ref, place.at_y())
            self.core[k, 0, step] = wires.put(ref, ref, place.at_core())

    def relay_plane(self, k):
        upper, lower = self.halves(k)
        place, wires, whole = self.place, self.wires, self.wholes[k]
        for step in range(self.steps):
            z = place.z_back(step)
            slot = place.slot(flip_x=1)
            ref = whole.at[z, slot]
            wires.landed(self.along_x[k, step], ref)
            half = whole.at[z, slot, upper]
            self.by_y[k, step] = wires.put(half, half, place.at_y())
            self.core[k, 1, step] = wires.put(ref, ref, place.at_core())
            slot = place.slot(flip_y=1)
            ref = whole.at[z, slot]
            wires.landed(self.along_y[k, step], ref)
            half = whole.at[z, slot, lower]
            self.by_x[k, step] = wires.put(half, half, place.at_x())
            self.core[k, 2, step] = wires.put(ref, ref, place.at_core())

    def relay_corner(self, k):
        upper, lower = self.halves(k)
        place, wires, whole = self.place, self.wires, self.wholes[k]
        slot = place.slot(flip_x=1, flip_y=1)
        for step in range(self.steps):
            z = place.z_back(step)
            wires.landed(self.by_y[k, step], whole.at[z, slot, upper])
            wires.landed(self.by_x[k, step], whole.at[z, slot, lower])
            ref = whole.at[z, slot]
            self.core[k, 3, step] = wires.put(ref, ref, place.at_core())

    def finish(self, k):
        place = self.place
        for part, (flip_y, flip_x) in enumerate(FLIPS):
            slot = place.slot(flip_y=flip_y, flip_c=1, flip_x=flip_x)
            for step in range(self.steps):
                ref = self.wholes[k].at[place.z_back(step), slot]
                self.wires.landed(self.core[k, part, step], ref)


class Scatter:
    def __init__(self, wires, place, grads, from_core, from_x, from_y, last_x, last_y, from_z):
        self.wires, self.place, self.grads = wires, place, grads
        self.from_core, self.from_x, self.from_y = from_core, from_x, from_y
        self.last_x, self.last_y, self.from_z = last_x, last_y, from_z
        self.steps = place.groups
        self.core, self.first, self.second, self.third = {}, {}, {}, {}

    def halves(self, k):
        some = SUMS_X[k]
        return pl.ds(0, some), pl.ds(some, SUMS[k] - some)

    def own(self, k, part, rows):
        flip_y, flip_x = FLIPS[part]
        return self.grads[k].at[:, self.place.slot(flip_y=flip_y, flip_x=flip_x), rows]

    def send_core(self, k):
        place = self.place
        for part in (3, 1, 2, 0):
            flip_y, flip_x = FLIPS[part]
            slot = place.slot(flip_y=flip_y, flip_c=1, flip_x=flip_x)
            self.core[k, part] = self.wires.put(
                self.grads[k].at[:, slot], self.from_core[k].at[part], place.at_core()
            )

    def add(self, into, other):
        def one(z, carry):
            total = into[z].astype(jnp.float32) + other[z].astype(jnp.float32)
            into[z] = total.astype(into.dtype)
            return carry

        lax.fori_loop(0, self.steps, one, 0)

    def after_core(self, k):
        upper, lower = self.halves(k)
        whole = pl.ds(0, SUMS[k])
        wires, place = self.wires, self.place
        for part in (3, 1, 2, 0):
            wires.landed(self.core[k, part], self.from_core[k].at[part])
            self.add(self.own(k, part, whole), self.from_core[k].at[part])
            if part == 3:
                self.first[k, "x", 1] = wires.put(
                    self.own(k, 3, upper), self.from_x[k].at[1], place.at_x()
                )
                self.first[k, "y", 1] = wires.put(
                    self.own(k, 3, lower), self.from_y[k].at[1], place.at_y()
                )
            elif part == 1:
                self.first[k, "x", 0] = wires.put(
                    self.own(k, 1, upper), self.from_x[k].at[0], place.at_x()
                )
            elif part == 2:
                self.first[k, "y", 0] = wires.put(
                    self.own(k, 2, lower), self.from_y[k].at[0], place.at_y()
                )

    def after_first(self, k):
        upper, lower = self.halves(k)
        wires, place = self.wires, self.place
        wires.landed(self.first[k, "x", 1], self.from_x[k].at[1])
        self.add(self.own(k, 2, upper), self.from_x[k].at[1])
        self.second[k, "y"] = wires.put(self.own(k, 2, upper), self.last_y[k], place.at_y())
        wires.landed(self.first[k, "y", 1], self.from_y[k].at[1])
        self.add(self.own(k, 1, lower), self.from_y[k].at[1])
        self.second[k, "x"] = wires.put(self.own(k, 1, lower), self.last_x[k], place.at_x())
        wires.landed(self.first[k, "x", 0], self.from_x[k].at[0])
        self.add(self.own(k, 0, upper), self.from_x[k].at[0])
        wires.landed(self.first[k, "y", 0], self.from_y[k].at[0])
        self.add(self.own(k, 0, lower), self.from_y[k].at[0])

    def after_second(self, k):
        upper, lower = self.halves(k)
        wires, place = self.wires, self.place
        wires.landed(self.second[k, "y"], self.last_y[k])
        self.add(self.own(k, 0, upper), self.last_y[k])
        wires.landed(self.second[k, "x"], self.last_x[k])
        self.add(self.own(k, 0, lower), self.last_x[k])
        for step in range(1, self.steps):
            z = place.z_of(step)
            self.third[k, step] = wires.put(
                self.grads[k].at[z, place.slot()], self.from_z[k].at[step - 1], place.at_z(step)
            )

    def finish(self, k):
        place = self.place
        total = self.grads[k][place.z, place.slot()].astype(jnp.float32)
        for step in range(1, self.steps):
            self.wires.landed(self.third[k, step], self.from_z[k].at[step - 1])
            total = total + self.from_z[k][step - 1].astype(jnp.float32)
        return total


def times(a, b):
    return lax.dot_general(a, b, (((1,), (0,)), ((), ())), preferred_element_type=jnp.float32)


def times_turned(a, b):
    return lax.dot_general(a, b, (((1,), (1,)), ((), ())), preferred_element_type=jnp.float32)


def turned_times(a, b):
    return lax.dot_general(a, b, (((0,), (0,)), ((), ())), preferred_element_type=jnp.float32)


def aligned(index, size):
    return pl.ds(pl.multiple_of(index * size, size), size)


def head_masks(lanes, head_dim):
    lane = lax.broadcasted_iota(jnp.int32, (1, lanes), 1)
    return [
        jnp.where((lane >= h * head_dim) & (lane < (h + 1) * head_dim), 1.0, 0.0).astype(jnp.bfloat16)
        for h in range(lanes // head_dim)
    ]


def gelu_and_slope(u):
    near = 1.0 / (1.0 + (0.3275911 * math.sqrt(0.5)) * jnp.abs(u))
    bell = jnp.exp(-0.5 * (u * u))
    series = near * (
        0.127414796
        + near * (-0.142248368 + near * (0.7107068705 + near * (-0.7265760135 + near * 0.5307027145)))
    )
    tail = series * bell
    below = jnp.where(u < 0.0, tail, 1.0 - tail)
    return u * below, below + u * (bell * (1.0 / math.sqrt(2.0 * math.pi)))


def assemble(source, first, blocks, target):
    per_z, size = source.shape[1] // 2, 24

    def one(i, carry):
        z, pair = lax.div(i, per_z), lax.rem(i, per_z)
        left = source[z, 2 * pair].astype(jnp.float32)
        right = source[z, 2 * pair + 1].astype(jnp.float32)
        for b in range(blocks):
            rows = slice(first + b * size, first + (b + 1) * size)
            both = jnp.concatenate([left[rows], right[rows]], axis=0)
            target[b, aligned(i, 2 * size), :] = both.astype(target.dtype)
        return carry

    lax.fori_loop(0, source.shape[0] * per_z, one, 0)


def sum_slabs(source, first):
    def one(i, total):
        per_z = source.shape[1]
        slab = source[lax.div(i, per_z), lax.rem(i, per_z)].astype(jnp.float32)
        return total + slab[first : first + 8]

    count = source.shape[0] * source.shape[1]
    return lax.fori_loop(0, count, one, jnp.zeros((8, source.shape[-1]), jnp.float32))


def normalize(row_data):
    center = row_data - jnp.mean(row_data, axis=-1, keepdims=True)
    spread = jnp.mean(center * center, axis=-1, keepdims=True)
    scale = lax.rsqrt(spread + EPS)
    return center * scale, scale


def weights_forward(queries, keys_all, live):
    scores = jnp.where(live, times_turned(queries, keys_all), -1e30)
    exponent = jnp.exp(scores - jnp.max(scores, axis=-1, keepdims=True))
    return (exponent * (1.0 / jnp.sum(exponent, axis=-1, keepdims=True))).astype(jnp.bfloat16)


def as_column(row):
    size = row.shape[1]
    down = lax.broadcasted_iota(jnp.int32, (size, size), 0)
    across = lax.broadcasted_iota(jnp.int32, (size, size), 1)
    return jnp.sum(jnp.where(down == across, row, 0.0), axis=1, keepdims=True)


def put_at(row, start, width):
    size = row.shape[1]
    down = lax.broadcasted_iota(jnp.int32, (size, width), 0)
    across = lax.broadcasted_iota(jnp.int32, (size, width), 1)
    return jnp.sum(jnp.where(across == down + start, as_column(row), 0.0), axis=0, keepdims=True)


def forward_kernel(
    short_len, long_len, w_qkv, w_out, w_up, w_down, qv_bias, out_bias, gains, shifts, up_bias,
    short_pool, long_pool, short_tok, long_tok,
    out_down, out_wq, out_wu, out_rows, out_qkv, out_short_probs, out_long_probs, out_mixed,
    out_first, out_hat, out_scale, out_low, out_acted, out_slope, vectors, share,
    whole0, whole1, whole2, wq, wu, rows_in, qkv, short_probs, long_probs, mixed,
    first, hat, scale, low, acted, slope, far_pool,
    send, recv, here, leave,
):
    place = Place()
    x, other = place.x, 1 - place.x
    short_rows, half = short_tok.shape[0], long_tok.shape[1]
    total_rows, width = rows_in.shape
    long_rows = 2 * half
    count, cap = short_pool.shape
    mine = pl.ds(pl.multiple_of(short_rows + x * half, half), half)
    theirs = pl.ds(pl.multiple_of(short_rows + other * half, half), half)
    local = []

    def move(src, dst):
        copy = pltpu.make_async_copy(src, dst, here.at[len(local)])
        copy.start()
        local.append(copy)
        return copy

    move(w_down, out_down.at[place.z, place.slot()])
    loads = [
        move(short_tok, rows_in.at[pl.ds(0, short_rows)]),
        move(long_tok.at[x], rows_in.at[mine]),
    ]
    place.greet_start()

    device = place.dp * 2 + x
    size = w_out.shape[0]

    def blocks(matrix):
        data = matrix[...].astype(jnp.float32)
        return [data[:, i * width : (i + 1) * width] for i in range(data.shape[1] // width)]

    pairs = [
        put_at(member[i : i + 1, :].astype(jnp.float32), device * size, width)
        for member in (qv_bias, out_bias, gains, shifts)
        for i in range(2)
    ]
    ups = put_at(up_bias[...].astype(jnp.float32), lax.rem(device, 8) * (4 * size), width)
    ups = jnp.where(lax.broadcasted_iota(jnp.int32, (8, 1), 0) == lax.div(device, 8), ups, 0.0)
    z, slot = place.z, place.slot()
    whole0[z, slot] = jnp.concatenate(blocks(w_qkv) + pairs, axis=0).astype(jnp.bfloat16)
    whole1[z, slot] = jnp.concatenate(blocks(w_out) + [ups], axis=0).astype(jnp.bfloat16)
    whole2[z, slot] = jnp.concatenate(blocks(w_up), axis=0).astype(jnp.bfloat16)

    place.greet_wait()
    wires = Wires(send, recv)
    net = Gather(wires, place, (whole0, whole1, whole2, out_down), w_down)
    net.start(0)
    net.start(1)
    net.start_plane(2)
    net.start(2)
    net.start_plane(1)
    net.start_plane(0)
    pooled = wires.put(long_pool, far_pool, place.at_x())
    net.relay_z(0)
    net.relay_plane(0)
    tok = wires.put(long_tok.at[other], rows_in.at[mine], place.at_x())
    net.relay_z(1)
    net.relay_corner(0)
    for copy in loads:
        copy.wait()
    net.finish(0)
    assemble(whole0, 0, 3, wq)
    vectors[0:8, :] = sum_slabs(whole0, 72)

    head_dim = width // HEADS
    score_scale = 1.0 / math.sqrt(head_dim)

    def project(i, carry):
        rows = aligned(i, 256)
        data = rows_in[rows, :]
        queries = times(data, wq[0]) + vectors[0:1, :]
        qkv[0, rows, :] = (queries.astype(jnp.bfloat16).astype(jnp.float32) * score_scale).astype(jnp.bfloat16)
        qkv[1, rows, :] = times(data, wq[1]).astype(jnp.bfloat16)
        qkv[2, rows, :] = (times(data, wq[2]) + vectors[1:2, :]).astype(jnp.bfloat16)
        return carry

    lax.fori_loop(0, short_rows // 256, project, 0)

    masks = head_masks(2 * head_dim, head_dim)
    keep_first = lax.broadcasted_iota(jnp.int32, (1, 2 * head_dim), 1) < head_dim
    place_in_block = lax.broadcasted_iota(jnp.int32, (1, cap), 1)
    short_live = [place_in_block < short_len[i] for i in range(count)]
    passage_len = long_len[x]
    long_live = lax.broadcasted_iota(jnp.int32, (1, long_rows), 1) < passage_len
    pairs = width // (2 * head_dim)

    def attend_short(pair, carry):
        lanes = aligned(pair, 2 * head_dim)
        blocks_of = [pl.ds(i * cap, cap) for i in range(count)]
        queries, keys_all, values = [[qkv[b, rows, lanes] for rows in blocks_of] for b in range(3)]
        units = [(i, h) for i in range(count) for h in range(2)]
        scores = [times_turned(queries[i] * masks[h], keys_all[i]) for i, h in units]
        scores = [jnp.where(short_live[i], part, -1e30) for (i, h), part in zip(units, scores)]
        tops = [jnp.max(part, axis=-1, keepdims=True) for part in scores]
        exponents = [jnp.exp(part - top) for part, top in zip(scores, tops)]
        totals = [jnp.sum(part, axis=-1, keepdims=True) for part in exponents]
        probs = [(part * (1.0 / total)).astype(jnp.bfloat16) for part, total in zip(exponents, totals)]
        parts = [times(part, values[i]) for (i, h), part in zip(units, probs)]
        for (i, h), part in zip(units, probs):
            short_probs[i, 2 * pair + h] = part
        for i in range(count):
            mixed[blocks_of[i], lanes] = jnp.where(keep_first, parts[2 * i], parts[2 * i + 1]).astype(jnp.bfloat16)
        return carry

    lax.fori_loop(0, pairs // 2, attend_short, 0)
    net.relay_z(2)
    lax.fori_loop(pairs // 2, pairs - 1, attend_short, 0)
    net.start(3)
    net.relay_plane(1)
    lax.fori_loop(pairs - 1, pairs, attend_short, 0)
    net.start_plane(3)
    move(short_probs, out_short_probs)
    wires.landed(tok, rows_in.at[theirs])
    lax.fori_loop(short_rows // 256, total_rows // 256, project, 0)
    move(qkv, out_qkv)
    move(rows_in, out_rows)

    wires.landed(pooled, far_pool)
    chosen = []
    for block in range(total_rows // cap):
        if block < count:
            mask, start = short_pool[block : block + 1, :], 0
            limit = short_len[block]
        else:
            step = block - count
            in_half, start = step % (half // cap) * cap, step * cap
            at = slice(in_half, in_half + cap)
            own = jnp.where(x == 0, long_pool[0:1, at], long_pool[1:2, at])
            far = jnp.where(x == 0, far_pool[0:1, at], far_pool[1:2, at])
            mask = jnp.where(x == step // (half // cap), own, far)
            limit = passage_len - start
        keep = (place_in_block < limit) & ((mask > 0) | (place_in_block + start == 0))
        chosen.append(jnp.where(keep, 1.0, 0.0))
    for block in range(count):
        share[block : block + 1, :] = chosen[block] / jnp.sum(chosen[block], axis=-1, keepdims=True)
    long_total = sum(jnp.sum(row, axis=-1, keepdims=True) for row in chosen[count:])
    for block in range(count, total_rows // cap):
        share[block : block + 1, :] = chosen[block] / long_total

    def attend_long(pair, carry):
        lanes = aligned(pair, 2 * head_dim)
        rows = pl.ds(short_rows, long_rows)
        keys_all, values = qkv[1, rows, lanes], qkv[2, rows, lanes]
        for block in range(long_rows // 256):
            inner = pl.ds(block * 256, 256)
            rows = pl.ds(short_rows + block * 256, 256)
            queries = qkv[0, rows, lanes]
            parts = []
            for h in range(2):
                probs = weights_forward(queries * masks[h], keys_all, long_live)
                long_probs[2 * pair + h, inner, :] = probs
                parts.append(times(probs, values))
            mixed[rows, lanes] = jnp.where(keep_first, parts[0], parts[1]).astype(jnp.bfloat16)
        return carry

    lax.fori_loop(0, pairs - 2, attend_long, 0)
    net.relay_plane(2)
    net.relay_corner(1)
    lax.fori_loop(pairs - 2, pairs - 1, attend_long, 0)
    net.relay_z(3)
    lax.fori_loop(pairs - 1, pairs, attend_long, 0)
    move(long_probs, out_long_probs)
    move(mixed, out_mixed)
    net.finish(1)
    assemble(whole1, 0, 1, wq.at[pl.ds(3, 1)])
    vectors[8:16, :] = sum_slabs(whole1, 24)
    move(wq, out_wq)

    def attach(i, carry):
        rows = aligned(i, 256)
        first_in = rows_in[rows, :].astype(jnp.float32) + (times(mixed[rows, :], wq[3]) + vectors[2:3, :])
        normal, factor = normalize(first_in)
        out = normal * vectors[4:5, :] + vectors[6:7, :]
        first[rows, :] = out
        low[rows, :] = out.astype(jnp.bfloat16)
        hat[rows, :] = normal.astype(jnp.bfloat16)
        scale[rows, :] = jnp.broadcast_to(factor, (256, scale.shape[1]))
        return carry

    lax.fori_loop(0, total_rows // 256, attach, 0)
    move(first, out_first)
    move(low, out_low)
    move(hat, out_hat)
    move(scale, out_scale)
    net.relay_corner(2)
    net.finish(2)
    assemble(whole2, 0, 4, wu)
    move(wu, out_wu)

    def leaving(i):
        j, rows = lax.div(i, 4), aligned(lax.rem(i, 4), 256)
        return (
            pltpu.make_async_copy(acted.at[j, rows], out_acted.at[j, rows], leave.at[0, i]),
            pltpu.make_async_copy(slope.at[j, rows], out_slope.at[j, rows], leave.at[1, i]),
        )

    def expand(i, carry):
        j, rows = lax.div(i, 4), aligned(lax.rem(i, 4), 256)
        inner = times(low[rows, :], wu[j]) + vectors[pl.ds(8 + j, 1), :]
        value, grad = gelu_and_slope(inner)
        acted[j, rows, :] = value.astype(jnp.bfloat16)
        slope[j, rows, :] = grad.astype(jnp.bfloat16)
        for copy in leaving(i):
            copy.start()
        return carry

    def left(i, carry):
        for copy in leaving(i):
            copy.wait()
        return carry

    lax.fori_loop(0, 7, expand, 0)
    net.relay_plane(3)
    lax.fori_loop(7, 14, expand, 0)
    net.relay_corner(3)
    lax.fori_loop(14, 16, expand, 0)
    net.finish(3)
    wires.close()
    lax.fori_loop(0, 16, left, 0)
    for copy in [local[0]] + local[3:]:
        copy.wait()


def forward(lengths, parameters, pools, short_tok, long_tok, groups):
    short_rows, width = short_tok.shape
    half = long_tok.shape[1]
    long_rows = 2 * half
    rows = short_rows + long_rows
    count, cap = pools[0].shape
    inner = 4 * width
    copies = 4 * ((groups - 1) + 4 * groups + 4 * groups) + 2
    low = jnp.bfloat16
    shape = jax.ShapeDtypeStruct
    outs = (
        shape((groups, 8, SIZES[3], width), low),
        shape((4, width, width), low),
        shape((4, width, width), low),
        shape((rows, width), low),
        shape((3, rows, width), low),
        shape((count, HEADS, cap, cap), low),
        shape((HEADS, long_rows, long_rows), low),
        shape((rows, width), low),
        shape((rows, width), jnp.float32),
        shape((rows, width), low),
        shape((rows, 128), jnp.float32),
        shape((rows, width), low),
        shape((inner // width, rows, width), low),
        shape((inner // width, rows, width), low),
        shape((16, width), jnp.float32),
        shape((rows // cap, cap), jnp.float32),
    )
    anywhere, near = pl.BlockSpec(memory_space=pl.ANY), pl.BlockSpec(memory_space=pltpu.VMEM)
    scalars = pl.BlockSpec(memory_space=pltpu.SMEM)
    kept = [pltpu.VMEM(out.shape, out.dtype) for out in outs[1:14]]
    return pl.pallas_call(
        forward_kernel,
        name="forward",
        out_shape=outs,
        in_specs=[scalars] * 2 + [near] * 11 + [anywhere] * 2,
        out_specs=[anywhere] * 14 + [near] * 2,
        scratch_shapes=[pltpu.VMEM((groups, 8, SIZES[k], width), low) for k in range(3)]
        + kept
        + [
            pltpu.VMEM(pools[1].shape, pools[1].dtype),
            pltpu.SemaphoreType.DMA((copies,)),
            pltpu.SemaphoreType.DMA((copies,)),
            pltpu.SemaphoreType.DMA((24,)),
            pltpu.SemaphoreType.DMA((2, 16)),
        ],
        compiler_params=pltpu.CompilerParams(
            collective_id=0, has_side_effects=True, vmem_limit_bytes=60 * 1024 * 1024
        ),
    )(*lengths, *parameters, *pools, short_tok, long_tok)


def backward_kernel(
    short_len, long_len, vectors, share, short_pool_cot, long_pool_cot, short_cot, long_cot,
    in_down, in_wq, in_wu, in_rows, in_qkv, in_short_probs, in_long_probs, in_mixed,
    in_first, in_hat, in_scale, in_low, in_acted, in_slope,
    short_out, long_out, short_grad, long_grad, short_pooled, long_pooled,
    grad_qkv, grad_out, grad_up, grad_down, grad_vectors, grad_up_vector,
    wide, pair, w_up, w_far, hat, sums, branch, low, scale, halves, probs_short,
    vector_sums, pool_cots, pooled_rows, pooled_own, pooled_far,
    *more,
):
    place = Place()
    x, other = place.x, 1 - place.x
    *chunks, send, recv, here, blocks, fetch = more
    parts = len(SUMS)
    grads, *received = [chunks[i * parts : (i + 1) * parts] for i in range(7)]
    total_rows, width = sums.shape
    short_rows = short_out.shape[0]
    count, cap = probs_short.shape[1], probs_short.shape[-1]
    long_rows = total_rows - short_rows
    half = long_rows // 2
    head_dim = width // HEADS
    steps = total_rows // 256
    low_type = jnp.bfloat16
    local = []

    def move(src, dst):
        copy = pltpu.make_async_copy(src, dst, here.at[len(local)])
        copy.start()
        local.append(copy)
        return copy

    mine = pl.ds(pl.multiple_of(short_rows + x * half, half), half)
    theirs = pl.ds(pl.multiple_of(short_rows + other * half, half), half)
    place.greet_start()
    load_down = [move(in_down.at[j], w_far.at[j]) for j in range(4)]
    load_down += [
        move(short_cot, branch.at[pl.ds(0, short_rows)]),
        move(long_cot.at[x], branch.at[mine]),
    ]
    passage_len = long_len[x]

    def block_at(step):
        return jnp.where(step < 2, step, 2 + lax.rem(step + x, 2))

    def block_copies(i):
        rows = aligned(i, 256)
        return (
            pltpu.make_async_copy(in_acted.at[:, rows], wide.at[:, rows], blocks.at[0, i]),
            pltpu.make_async_copy(in_first.at[rows], sums.at[rows], blocks.at[1, i]),
        )

    for copy in block_copies(0):
        copy.start()
    vector_sums[...] = jnp.zeros_like(vector_sums)
    pool_cots[0:count, :] = short_pool_cot[...]
    pool_cots[count : 2 * count, :] = jnp.broadcast_to(long_pool_cot[pl.ds(x, 1), :], (count, width))
    place.greet_wait()
    wires = Wires(send, recv)
    swap_cot = wires.put(long_cot.at[other], branch.at[mine], place.at_x())
    net = Scatter(wires, place, grads, *received)
    for copy in load_down:
        copy.wait()
    tall = lax.broadcasted_iota(jnp.int32, (256, 1), 0)
    diagonal = lax.broadcasted_iota(jnp.int32, (cap, cap), 0) == lax.broadcasted_iota(jnp.int32, (cap, cap), 1)

    def add_vector(row, rows):
        vector_sums[row : row + 1, :] += jnp.sum(rows, axis=0, keepdims=True)

    def second(step, carry):
        i = block_at(step)
        rows = aligned(i, 256)

        @pl.when(step == steps - 1)
        def _():
            wires.landed(swap_cot, branch.at[theirs])

        @pl.when(step < steps - 1)
        def _():
            for copy in block_copies(block_at(step + 1)):
                copy.start()

        for copy in block_copies(i):
            copy.wait()
        product = times(wide[0, rows, :], w_far[0])
        for j in range(1, 4):
            product += times(wide[j, rows, :], w_far[j])
        normal, factor = normalize(sums[rows, :] + (product + vectors[3:4, :]))
        lens = [
            jnp.where(2 * i + part < count, short_len[lax.rem(2 * i + part, count)], passage_len - (2 * i + part - count) * cap)
            for part in range(2)
        ]
        live = tall < jnp.where(tall < cap, lens[0], lens[1] + cap)
        final = jnp.where(live, normal * vectors[5:6, :] + vectors[7:8, :], 0.0)
        low[rows, :] = final.astype(low_type)
        spread = []
        for part in range(2):
            share_row = share[pl.ds(2 * i + part, 1), :]
            column = jnp.sum(jnp.where(diagonal, share_row, 0.0), axis=1, keepdims=True)
            piece = final[part * cap : (part + 1) * cap]
            pooled_rows[pl.ds(2 * i + part, 1), :] = jnp.sum(piece * column, axis=0, keepdims=True)
            spread.append(column * pool_cots[pl.ds(2 * i + part, 1), :])
        grad_final = jnp.where(live, branch[rows, :].astype(jnp.float32), 0.0) + jnp.concatenate(spread, axis=0)
        add_vector(5, grad_final * normal)
        add_vector(7, grad_final)
        scaled = grad_final * vectors[5:6, :]
        mean_one = jnp.mean(scaled, axis=-1, keepdims=True)
        mean_two = jnp.mean(scaled * normal, axis=-1, keepdims=True)
        grad_second = factor * (scaled - mean_one - normal * mean_two)
        sums[rows, :] = grad_second
        grad_branch = grad_second.astype(low_type)
        branch[rows, :] = grad_branch
        add_vector(3, grad_branch.astype(jnp.float32))
        return carry

    lax.fori_loop(0, steps, second, 0)
    short_pooled[...] = pooled_rows[0:count, :]
    own_pooled = jnp.sum(pooled_rows[count : 2 * count, :], axis=0, keepdims=True)
    pooled_own[...] = jnp.broadcast_to(own_pooled, pooled_own.shape)
    long_pooled[pl.ds(x, 1), :] = own_pooled
    out_copies = [
        move(low.at[pl.ds(0, short_rows)], short_out),
        move(low.at[mine], long_out.at[x]),
    ]
    load_slope = [move(in_slope.at[0], pair.at[0]), move(in_slope.at[1], pair.at[1])]
    load_up = move(in_wu, w_up)
    load_hat, load_scale = move(in_hat, hat), move(in_scale, scale)

    swap_out = wires.put(low.at[theirs], long_out.at[x], place.at_x())
    swap_pooled = wires.put(pooled_own, pooled_far, place.at_x())

    def down_step(i, carry):
        j, part = lax.div(i, 2), lax.rem(i, 2)
        product = turned_times(wide[j, :, aligned(part, width // 2)], branch[...])
        grads[5][j, aligned(part, 4)] = product.reshape(4, SUMS[5], width).astype(low_type)
        return carry

    lax.fori_loop(0, 8, down_step, 0, unroll=2)
    net.send_core(5)

    def inner_block(j):
        def inner(i, carry):
            rows = aligned(i, 256)
            product = times_turned(branch[rows, :], w_far[j]) * pair[j % 2, rows, :].astype(jnp.float32)
            grad_inner = product.astype(low_type)
            wide[j, rows, :] = grad_inner
            add_vector(8 + j, grad_inner.astype(jnp.float32))
            return carry

        lax.fori_loop(0, steps, inner, 0, unroll=2)

    load_slope[0].wait()
    inner_block(0)
    load_slope.append(move(in_slope.at[2], pair.at[0]))
    load_slope[1].wait()
    inner_block(1)
    load_slope.append(move(in_slope.at[3], pair.at[1]))
    for copy in out_copies:
        copy.wait()
    wires.has_left(swap_out)
    load_low = move(in_low, low)
    net.after_core(5)
    load_slope[2].wait()
    inner_block(2)
    load_mixed = move(in_mixed, pair.at[0])
    load_slope[3].wait()
    inner_block(3)
    load_wq = move(in_wq, w_far)

    def up_step(i, carry):
        r, both = lax.div(i, 2), lax.rem(i, 2)
        data = low[:, aligned(r, width // 2)]
        halves[0] = turned_times(data, wide[2 * both])
        halves[1] = turned_times(data, wide[2 * both + 1])

        def one(k, carry):
            rows = pl.ds(pl.multiple_of(k * 24, 8), 24)
            data = jnp.concatenate([halves[0, rows, :], halves[1, rows, :]], axis=0)
            grads[4][2 * r + lax.div(k, 8), lax.rem(k, 8), aligned(both, 48), :] = data.astype(low_type)
            return carry

        return lax.fori_loop(0, 16, one, carry)

    load_low.wait()
    lax.fori_loop(0, 4, up_step, 0)
    net.send_core(4)
    net.after_first(5)

    load_up.wait()
    load_hat.wait()
    load_scale.wait()

    def first_back(i, carry):
        rows = aligned(i, 256)
        grad_first = sums[rows, :]
        for j in range(4):
            grad_first += times_turned(wide[j, rows, :], w_up[j])
        normal = hat[rows, :].astype(jnp.float32)
        add_vector(4, grad_first * normal)
        add_vector(6, grad_first)
        scaled = grad_first * vectors[4:5, :]
        mean_one = jnp.mean(scaled, axis=-1, keepdims=True)
        mean_two = jnp.mean(scaled * normal, axis=-1, keepdims=True)
        grad_in = scale[rows, 0:1] * (scaled - mean_one - normal * mean_two)
        sums[rows, :] = grad_in
        grad_attn = grad_in.astype(low_type)
        branch[rows, :] = grad_attn
        add_vector(2, grad_attn.astype(jnp.float32))
        return carry

    lax.fori_loop(0, steps // 2, first_back, 0)
    net.after_core(4)
    lax.fori_loop(steps // 2, steps, first_back, 0)
    load_qkv = move(in_qkv, wide.at[pl.ds(0, 3)])
    load_rows = move(in_rows, wide.at[3])
    net.after_second(5)

    load_mixed.wait()
    load_wq.wait()
    def out_step(r, carry):
        halves[0] = turned_times(pair[0, :, aligned(r, width // 2)], branch[...])

        def one(k, carry):
            rows = pl.ds(pl.multiple_of(k * 24, 8), 24)
            data = jnp.concatenate([halves[0, rows, :], vector_sums[8:16, :]], axis=0)
            grads[3][2 * r + lax.div(k, 8), lax.rem(k, 8)] = data.astype(low_type)
            return carry

        return lax.fori_loop(0, 16, one, carry)

    lax.fori_loop(0, 2, out_step, 0)

    def mixed_back(i, carry):
        rows = aligned(i, 256)
        pair[1, rows, :] = times_turned(branch[rows, :], w_far[3]).astype(low_type)
        return carry

    lax.fori_loop(0, steps, mixed_back, 0)
    net.send_core(3)

    def probs_copies(p, slot):
        lanes = pl.ds(2 * p, 2)
        return (
            pltpu.make_async_copy(in_short_probs.at[:, lanes], probs_short.at[slot], fetch.at[0, slot]),
            pltpu.make_async_copy(
                in_long_probs.at[lanes],
                w_up.at[pl.ds(2 * slot, 2), pl.ds(0, long_rows), pl.ds(0, long_rows)],
                fetch.at[1, slot],
            ),
        )

    for copy in probs_copies(0, 0):
        copy.start()
    load_qkv.wait()
    score_scale = 1.0 / math.sqrt(head_dim)
    masks = head_masks(2 * head_dim, head_dim)
    pairs = width // (2 * head_dim)

    def attend_back(lanes, units):
        heads = [(u, h) for u in range(len(units)) for h in range(2)]
        queries = [wide[0, rows, lanes] for rows, _, _, _ in units]
        grads_mixed = [pair[1, rows, lanes] for rows, _, _, _ in units]
        overlaps = [
            grad.astype(jnp.float32) * pair[0, rows, lanes].astype(jnp.float32)
            for grad, (rows, _, _, _) in zip(grads_mixed, units)
        ]
        centers = [
            jnp.sum(overlaps[u] * masks[h].astype(jnp.float32), axis=-1, keepdims=True) for u, h in heads
        ]
        grads_head = [grads_mixed[u] * masks[h] for u, h in heads]
        probs = [units[u][1](h) for u, h in heads]
        grads_probs = [times_turned(grad, units[u][3]) for grad, (u, h) in zip(grads_head, heads)]
        scores = [
            (part.astype(jnp.float32) * (grad - center)).astype(low_type)
            for part, grad, center in zip(probs, grads_probs, centers)
        ]
        grads_q = [times(part, units[u][2] * masks[h]) for part, (u, h) in zip(scores, heads)]
        grads_k = [turned_times(queries[u] * masks[h], part) for part, (u, h) in zip(scores, heads)]
        grads_v = [turned_times(grad, part) for part, grad in zip(probs, grads_head)]
        for u, (rows, _, _, _) in enumerate(units):
            total = grads_q[2 * u] + grads_q[2 * u + 1]
            wide[0, rows, lanes] = (total * score_scale).astype(low_type)
        return [
            [grads[2 * u] + grads[2 * u + 1] for u in range(len(units))] for grads in (grads_k, grads_v)
        ]

    def attention_back(p, carry):
        slot = lax.rem(p, 2)
        for copy in probs_copies(p, slot):
            copy.wait()

        @pl.when(p + 1 < pairs)
        def _():
            for copy in probs_copies(p + 1, 1 - slot):
                copy.start()

        lanes = aligned(p, 2 * head_dim)
        blocks_of = [pl.ds(i * cap, cap) for i in range(count)]
        units = [
            (rows, lambda h, i=i: probs_short[slot, i, h], wide[1, rows, lanes], wide[2, rows, lanes])
            for i, rows in enumerate(blocks_of)
        ]
        grads_k, grads_v = attend_back(lanes, units)
        for rows, grad_k, grad_v in zip(blocks_of, grads_k, grads_v):
            wide[1, rows, lanes] = grad_k.T.astype(low_type)
            wide[2, rows, lanes] = grad_v.T.astype(low_type)
        rows = pl.ds(short_rows, long_rows)
        keys_all, values = wide[1, rows, lanes], wide[2, rows, lanes]
        total_k, total_v = None, None
        for block in range(long_rows // 256):
            inner = pl.ds(block * 256, 256)
            unit = (
                pl.ds(short_rows + block * 256, 256),
                lambda h, inner=inner: w_up[2 * slot + h, inner, 0:long_rows],
                keys_all,
                values,
            )
            (grad_k,), (grad_v,) = attend_back(lanes, [unit])
            total_k = grad_k if total_k is None else total_k + grad_k
            total_v = grad_v if total_v is None else total_v + grad_v
        wide[1, rows, lanes] = total_k.T.astype(low_type)
        wide[2, rows, lanes] = total_v.T.astype(low_type)
        return carry

    third = width // 3

    def qkv_step(group):
        lanes = pl.ds(group * third, third)

        def bias(i, carry):
            rows = aligned(i, 256)
            for row, b in ((0, 0), (1, 2)):
                piece = wide[b, rows, lanes].astype(jnp.float32)
                vector_sums[row : row + 1, lanes] += jnp.sum(piece, axis=0, keepdims=True)
            return carry

        lax.fori_loop(0, steps, bias, 0)

        def step(r, carry):
            data = wide[3, :, aligned(r, width // 2)]
            for b in range(3):
                halves[0, :, b * third : (b + 1) * third] = turned_times(data, wide[b, :, lanes])

            def one(k, carry):
                rows = pl.ds(pl.multiple_of(k * 24, 8), 24)
                pieces = [halves[0, rows, b * third : (b + 1) * third] for b in range(3)]
                data = jnp.concatenate(pieces + [vector_sums[0:8, lanes]], axis=0)
                grads[group][2 * r + lax.div(k, 8), lax.rem(k, 8)] = data.astype(low_type)
                return carry

            return lax.fori_loop(0, 16, one, carry)

        lax.fori_loop(0, 2, step, 0)

    lax.fori_loop(0, pairs // 3, attention_back, 0)
    net.after_first(4)
    load_rows.wait()
    qkv_step(0)
    net.after_core(3)
    net.send_core(0)
    lax.fori_loop(pairs // 3, 2 * pairs // 3, attention_back, 0)
    net.after_second(4)
    net.after_core(0)
    qkv_step(1)
    net.send_core(1)
    net.after_first(3)
    lax.fori_loop(2 * pairs // 3, pairs, attention_back, 0)
    net.after_core(1)
    net.after_first(0)
    qkv_step(2)
    net.send_core(2)
    net.after_second(3)

    def tokens_back(rows):
        grad_in = sums[rows, :]
        for b in range(3):
            grad_in += times_turned(wide[b, rows, :], w_far[b])
        return grad_in

    far_low, far_in = low.at[pl.ds(0, half)], low.at[pl.ds(half, half)]
    far_low[...] = tokens_back(theirs).astype(low_type)

    def tokens_step(i, carry):
        rows = pl.ds(pl.multiple_of(jnp.where(i < 2, i * 256, short_rows + x * half), 256), 256)
        sums[rows, :] = tokens_back(rows)
        return carry

    lax.fori_loop(0, 1, tokens_step, 0)
    net.after_core(2)
    net.after_first(1)
    net.after_second(0)
    net.after_first(2)
    swap_grad = wires.put(far_low, far_in, place.at_x())
    net.after_second(1)
    net.after_second(2)
    lax.fori_loop(1, 3, tokens_step, 0)
    move(sums.at[pl.ds(0, short_rows)], short_grad)
    move(sums.at[mine], long_grad.at[x])
    grad_down[...] = net.finish(5)
    total = net.finish(4)
    for j in range(4):
        grad_up[:, j * width : (j + 1) * width] = total[24 * j : 24 * j + 24]
    total = net.finish(3)
    grad_out[...] = total[0:24]
    grad_up_vector[...] = total[24:32]
    wires.landed(swap_pooled, pooled_far)
    long_pooled[pl.ds(other, 1), :] = pooled_far[0:1, :]
    wires.landed(swap_grad, far_in)
    sums[theirs, :] = far_in[...].astype(jnp.float32)
    move(sums.at[theirs], long_grad.at[other])
    wires.landed(swap_out, long_out.at[other])
    for group in range(3):
        total = net.finish(group)
        for b in range(3):
            columns = slice(b * width + group * third, b * width + (group + 1) * third)
            grad_qkv[:, columns] = total[24 * b : 24 * b + 24]
        grad_vectors[:, group * third : (group + 1) * third] = total[72:80]
    wires.close()
    for copy in local[-3:]:
        copy.wait()


def backward(lengths, vectors, share, pool_cots, cots, arrays, groups):
    width = vectors.shape[1]
    rows = arrays[3].shape[0]
    count, _, cap, _ = arrays[5].shape
    short_rows = count * cap
    half = (rows - short_rows) // 2
    low, wide_type = jnp.bfloat16, jnp.float32
    shape = jax.ShapeDtypeStruct
    rows24 = 24
    outs = (
        shape((short_rows, width), low),
        shape((2, half, width), low),
        shape((short_rows, width), wide_type),
        shape((2, half, width), wide_type),
        shape((count, width), wide_type),
        shape((2, width), wide_type),
        shape((rows24, 3 * width), wide_type),
        shape((rows24, width), wide_type),
        shape((rows24, 4 * width), wide_type),
        shape((4 * rows24, width), wide_type),
        shape((8, width), wide_type),
        shape((8, width), wide_type),
    )
    anywhere, near = pl.BlockSpec(memory_space=pl.ANY), pl.BlockSpec(memory_space=pltpu.VMEM)
    copies = len(SUMS) * (4 + 6 + (groups - 1)) + 4

    widths = (width // 3,) * 3 + (width,) * 3

    def chunks(parts, sizes):
        return [pltpu.VMEM(parts + (size, columns), low) for size, columns in zip(sizes, widths)]

    rest = tuple(size - some for size, some in zip(SUMS, SUMS_X))
    scratch = [
        pltpu.VMEM((4, rows, width), low),
        pltpu.VMEM((2, rows, width), low),
        pltpu.VMEM((4, width, width), low),
        pltpu.VMEM((4, width, width), low),
        pltpu.VMEM((rows, width), low),
        pltpu.VMEM((rows, width), wide_type),
        pltpu.VMEM((rows, width), low),
        pltpu.VMEM((rows, width), low),
        pltpu.VMEM((rows, 128), wide_type),
        pltpu.VMEM((2, width // 2, width), wide_type),
        pltpu.VMEM((2, count, 2, cap, cap), low),
        pltpu.VMEM((16, width), wide_type),
        pltpu.VMEM((2 * count, width), wide_type),
        pltpu.VMEM((2 * count, width), wide_type),
        pltpu.VMEM((8, width), wide_type),
        pltpu.VMEM((8, width), wide_type),
        *chunks((groups, 8), SUMS),
        *chunks((4, groups), SUMS),
        *chunks((2, groups), SUMS_X),
        *chunks((2, groups), rest),
        *chunks((groups,), rest),
        *chunks((groups,), SUMS_X),
        *chunks((groups - 1,), SUMS),
        pltpu.SemaphoreType.DMA((copies,)),
        pltpu.SemaphoreType.DMA((copies,)),
        pltpu.SemaphoreType.DMA((24,)),
        pltpu.SemaphoreType.DMA((2, rows // 256)),
        pltpu.SemaphoreType.DMA((2, 2)),
    ]
    return pl.pallas_call(
        backward_kernel,
        name="backward",
        out_shape=outs,
        in_specs=[pl.BlockSpec(memory_space=pltpu.SMEM)] * 2 + [near] * 4 + [anywhere] * 16,
        out_specs=[anywhere] * 4 + [near] * 8,
        scratch_shapes=scratch,
        compiler_params=pltpu.CompilerParams(
            collective_id=1, has_side_effects=True, vmem_limit_bytes=63 * 1024 * 1024
        ),
    )(*lengths, vectors, share, *pool_cots, *cots, *arrays)


def results_kernel(
    in_0, in_1, in_2, in_3, in_4, in_5, in_6, in_7, in_8, in_9, grad_vectors, grad_ups,
    out_0, out_1, out_2, out_3, out_4, out_5, out_6, out_7, out_8, out_9, pair_0, pair_1, ups, pair_2, pair_3,
    *more,
):
    *held, come, leave = more
    sources = (in_0, in_1, in_2, in_3, in_4, in_5, in_6, in_7, in_8, in_9)
    places = (out_0, out_1, out_4, out_5, out_2, out_3, out_6, out_7, out_8, out_9)
    ins = [pltpu.make_async_copy(sources[i], held[i], come.at[i]) for i in range(10)]
    outs = [pltpu.make_async_copy(held[i], places[i], leave.at[i]) for i in range(10)]
    for copy in ins:
        copy.start()
    device = lax.axis_index("dp") * 2 + lax.axis_index("seq")
    size, width = in_7.shape
    rows = pltpu.roll(grad_vectors[...], lax.rem(width - device * size, width), 1)
    for i, ref in enumerate((pair_0, pair_1, pair_2, pair_3)):
        ref[...] = rows[2 * i : 2 * i + 2, 0:size]
    start = lax.rem(device, 8) * (4 * size)
    row = grad_ups[pl.ds(lax.div(device, 8), 1), :]
    row = pltpu.roll(jnp.broadcast_to(row, (8, width)), lax.rem(width - start, width), 1)
    ups[...] = row[0:1, 0 : 4 * size]
    for i in range(10):
        ins[i].wait()
        outs[i].start()
    for copy in outs:
        copy.wait()


def results(arrays):
    size = arrays[7].shape[0]
    order = (0, 1, 4, 5, 2, 3, 6, 7, 8, 9)
    shape = jax.ShapeDtypeStruct
    pair = shape((2, size), jnp.float32)
    outs = tuple(shape(arrays[i].shape, arrays[i].dtype) for i in order)
    anywhere, near = pl.BlockSpec(memory_space=pl.ANY), pl.BlockSpec(memory_space=pltpu.VMEM)
    return pl.pallas_call(
        results_kernel,
        name="results",
        out_shape=outs + (pair, pair, shape((1, 4 * size), jnp.float32), pair, pair),
        in_specs=[anywhere] * 10 + [near] * 2,
        out_specs=[anywhere] * 10 + [near] * 5,
        scratch_shapes=[pltpu.VMEM(array.shape, array.dtype) for array in arrays[:10]]
        + [pltpu.SemaphoreType.DMA((10,)), pltpu.SemaphoreType.DMA((10,))],
        compiler_params=pltpu.CompilerParams(vmem_limit_bytes=56 * 1024 * 1024),
    )(*arrays)


def layer_norm(row_data, gain_vec, shift_vec):
    center = row_data - jnp.mean(row_data, axis=-1, keepdims=True)
    spread = jnp.mean(center * center, axis=-1, keepdims=True)
    return center * lax.rsqrt(spread + EPS) * gain_vec + shift_vec


def exact_gelu(inner_act):
    return jax.nn.gelu(inner_act, approximate=False)


def outer_sum(left_rows, right_rows):
    return lax.dot_general(
        left_rows, right_rows, (((0,), (0,)), ((), ())), preferred_element_type=jnp.float32
    )


def times_transposed(left_rows, matrix):
    return lax.dot_general(
        left_rows, matrix, (((1,), (1,)), ((), ())), preferred_element_type=jnp.float32
    )


def masked_scores(queries, keys_all, key_live, score_scale):
    scores = (
        jnp.einsum("bqhe,bkhe->bhqk", queries, keys_all, preferred_element_type=jnp.float32)
        * score_scale
    )
    return jnp.where(key_live[:, None, None, :], scores, -1e30)


def attend_forward(pieces, score_scale):
    queries, keys_all, values, key_live = pieces
    scores = masked_scores(queries, keys_all, key_live, score_scale)
    highest = jnp.max(scores, axis=-1, keepdims=True)
    exponent = jnp.exp(scores - highest)
    totals = jnp.sum(exponent, axis=-1, keepdims=True)
    soft_probs = (exponent / totals).astype(jnp.bfloat16)
    mixed_heads = jnp.einsum(
        "bhqk,bkhe->bqhe", soft_probs, values, preferred_element_type=jnp.float32
    )
    return (mixed_heads.astype(jnp.bfloat16), (highest + jnp.log(totals))[..., 0])


def attend_backward(pieces, score_scale):
    queries, keys_all, values, key_live, grad_mixed, log_total = pieces
    scores = masked_scores(queries, keys_all, key_live, score_scale)
    soft_probs = jnp.exp(scores - log_total[..., None])
    grad_probs = jnp.einsum(
        "bqhe,bkhe->bhqk", grad_mixed, values, preferred_element_type=jnp.float32
    )
    grad_values = jnp.einsum(
        "bhqk,bqhe->bkhe",
        soft_probs.astype(jnp.bfloat16),
        grad_mixed,
        preferred_element_type=jnp.float32,
    )
    center = jnp.sum(soft_probs * grad_probs, axis=-1, keepdims=True)
    grad_scores = (soft_probs * (grad_probs - center)).astype(jnp.bfloat16)
    grad_queries = (
        jnp.einsum("bhqk,bkhe->bqhe", grad_scores, keys_all, preferred_element_type=jnp.float32)
        * score_scale
    )
    grad_keys = (
        jnp.einsum("bhqk,bqhe->bkhe", grad_scores, queries, preferred_element_type=jnp.float32)
        * score_scale
    )
    return (grad_queries, grad_keys, grad_values)


def by_blocks(function, per_block, arrays):
    blocks = arrays[0].shape[0] // per_block
    stacked = tuple((member.reshape((blocks, per_block) + member.shape[1:]) for member in arrays))
    results = lax.map(function, stacked)
    return jax.tree.map(
        lambda member: member.reshape((blocks * per_block,) + member.shape[2:]), results
    )


def general_shards(
    short_tokens,
    long_tokens,
    short_len,
    long_len,
    short_pool,
    long_pool,
    short_cot,
    long_cot,
    short_pool_cot,
    long_pool_cot,
    w_qkv,
    w_out,
    w_up,
    w_down,
    qv_bias,
    out_bias,
    up_bias,
    norm_gain,
    norm_shift,
):
    gathered = (
        lax.all_gather(w_qkv, ("dp", "seq"), axis=0, tiled=True),
        lax.all_gather(w_out, ("dp", "seq"), axis=0, tiled=True),
        lax.all_gather(w_up, ("dp", "seq"), axis=0, tiled=True),
        lax.all_gather(w_down, ("dp", "seq"), axis=0, tiled=True),
        lax.all_gather(qv_bias, ("dp", "seq"), axis=0, tiled=True),
        lax.all_gather(out_bias, ("dp", "seq"), axis=0, tiled=True),
        lax.all_gather(up_bias, ("dp", "seq"), axis=0, tiled=True),
        lax.all_gather(norm_gain, ("dp", "seq"), axis=0, tiled=True),
        lax.all_gather(norm_shift, ("dp", "seq"), axis=0, tiled=True),
    )
    qkv_matrix, out_matrix, up_matrix, down_matrix, qv_vec, out_vec, up_vec, gains, shifts = (
        gathered
    )
    gains = gains.astype(jnp.float32)
    shifts = shifts.astype(jnp.float32)
    short_count, short_cap, model_width = short_tokens.shape
    long_count, long_half = (long_tokens.shape[0], long_tokens.shape[1])
    head_count = HEADS
    head_dim = model_width // head_count
    score_scale = 1.0 / math.sqrt(head_dim)
    short_rows = short_count * short_cap
    long_rows = long_count * long_half
    short_place = jnp.arange(short_cap, dtype=jnp.int32)
    short_live = short_place[None, :] < short_len[:, None]
    long_place = lax.axis_index("seq") * long_half + jnp.arange(long_half, dtype=jnp.int32)
    long_live = long_place[None, :] < long_len[:, None]
    short_weight = (short_live & ((short_pool > 0) | (short_place[None, :] == 0))).astype(
        jnp.float32
    )
    long_weight = (long_live & ((long_pool > 0) | (long_place[None, :] == 0))).astype(jnp.float32)
    row_live = jnp.concatenate([short_live.reshape(-1), long_live.reshape(-1)]).astype(jnp.float32)
    inputs = jnp.concatenate(
        [
            short_tokens.reshape(short_rows, model_width),
            long_tokens.reshape(long_rows, model_width),
        ],
        axis=0,
    )
    joined = jnp.dot(inputs, qkv_matrix, preferred_element_type=jnp.float32)
    queries = (joined[:, :model_width] + qv_vec[:, 0]).astype(jnp.bfloat16)
    keys_all = joined[:, model_width : 2 * model_width].astype(jnp.bfloat16)
    values = (joined[:, 2 * model_width :] + qv_vec[:, 1]).astype(jnp.bfloat16)
    short_shape = (short_count, short_cap, head_count, head_dim)
    long_shape = (long_count, long_half, head_count, head_dim)
    short_q = queries[:short_rows].reshape(short_shape)
    short_k = keys_all[:short_rows].reshape(short_shape)
    short_v = values[:short_rows].reshape(short_shape)
    long_q = queries[short_rows:].reshape(long_shape)
    long_k = keys_all[short_rows:].reshape(long_count, long_half, model_width)
    long_v = values[short_rows:].reshape(long_count, long_half, model_width)
    short_block = math.gcd(short_count, max(1, 512 // short_cap))
    long_block = math.gcd(long_count, max(1, 512 // long_half))

    def forward_blocks(pieces):
        return attend_forward(pieces, score_scale)

    def backward_blocks(pieces):
        return attend_backward(pieces, score_scale)

    short_mixed, short_logsum = by_blocks(
        forward_blocks, short_block, (short_q, short_k, short_v, short_live)
    )
    gathered_k, gathered_v = (
        lax.all_gather(long_k, "seq", axis=1, tiled=True),
        lax.all_gather(long_v, "seq", axis=1, tiled=True),
    )
    full_len = gathered_k.shape[1]
    full_shape = (long_count, full_len, head_count, head_dim)
    long_key_live = jnp.arange(full_len, dtype=jnp.int32)[None, :] < long_len[:, None]
    long_mixed, long_logsum = by_blocks(
        forward_blocks,
        long_block,
        (long_q, gathered_k.reshape(full_shape), gathered_v.reshape(full_shape), long_key_live),
    )
    mixed_heads = jnp.concatenate(
        [short_mixed.reshape(short_rows, model_width), long_mixed.reshape(long_rows, model_width)],
        axis=0,
    )
    attn_out = jnp.dot(mixed_heads, out_matrix, preferred_element_type=jnp.float32) + out_vec[:, 0]
    first_in = inputs.astype(jnp.float32) + attn_out
    first_norm = layer_norm(first_in, gains[:, 0], shifts[:, 0])
    first_low = first_norm.astype(jnp.bfloat16)
    inner_act = jnp.dot(first_low, up_matrix, preferred_element_type=jnp.float32) + up_vec
    activated = exact_gelu(inner_act).astype(jnp.bfloat16)
    branch = jnp.dot(activated, down_matrix, preferred_element_type=jnp.float32) + out_vec[:, 1]
    second_in = first_norm + branch
    final_norm = layer_norm(second_in, gains[:, 1], shifts[:, 1]) * row_live[:, None]
    short_final = final_norm[:short_rows].reshape(short_count, short_cap, model_width)
    long_final = final_norm[short_rows:].reshape(long_count, long_half, model_width)
    short_total = jnp.sum(short_weight, axis=1)
    short_pooled = jnp.sum(short_final * short_weight[..., None], axis=1) / short_total[:, None]
    long_partial = jnp.sum(long_final * long_weight[..., None], axis=1)
    long_sum, long_total = lax.psum((long_partial, jnp.sum(long_weight, axis=1)), "seq")
    long_pooled = long_sum / long_total[:, None]
    grad_short = (
        short_cot.astype(jnp.float32) * short_live[..., None]
        + short_weight[..., None] * short_pool_cot[:, None, :] / short_total[:, None, None]
    )
    grad_long = (
        long_cot.astype(jnp.float32) * long_live[..., None]
        + long_weight[..., None] * long_pool_cot[:, None, :] / long_total[:, None, None]
    )
    grad_top = jnp.concatenate(
        [grad_short.reshape(short_rows, model_width), grad_long.reshape(long_rows, model_width)],
        axis=0,
    )
    _, second_back = jax.vjp(layer_norm, second_in, gains[:, 1], shifts[:, 1])
    grad_second, grad_gain_two, grad_shift_two = second_back(grad_top)
    grad_branch = grad_second.astype(jnp.bfloat16)
    grad_down = outer_sum(activated, grad_branch)
    grad_bias_two = jnp.sum(grad_branch.astype(jnp.float32), axis=0)
    grad_acted = times_transposed(grad_branch, down_matrix)
    _, gelu_back = jax.vjp(exact_gelu, inner_act)
    grad_inner = gelu_back(grad_acted)[0].astype(jnp.bfloat16)
    grad_up = outer_sum(first_low, grad_inner)
    grad_up_bias = jnp.sum(grad_inner.astype(jnp.float32), axis=0)
    grad_first = grad_second + times_transposed(grad_inner, up_matrix)
    _, first_back = jax.vjp(layer_norm, first_in, gains[:, 0], shifts[:, 0])
    grad_first_in, grad_gain_one, grad_shift_one = first_back(grad_first)
    grad_attn = grad_first_in.astype(jnp.bfloat16)
    grad_out = outer_sum(mixed_heads, grad_attn)
    grad_bias_one = jnp.sum(grad_attn.astype(jnp.float32), axis=0)
    grad_mixed = times_transposed(grad_attn, out_matrix).astype(jnp.bfloat16)
    short_dq, short_dk, short_dv = by_blocks(
        backward_blocks,
        short_block,
        (
            short_q,
            short_k,
            short_v,
            short_live,
            grad_mixed[:short_rows].reshape(short_shape),
            short_logsum,
        ),
    )
    again_k, again_v = (gathered_k, gathered_v)
    long_dq, long_dk, long_dv = by_blocks(
        backward_blocks,
        long_block,
        (
            long_q,
            again_k.reshape(full_shape),
            again_v.reshape(full_shape),
            long_key_live,
            grad_mixed[short_rows:].reshape(long_shape),
            long_logsum,
        ),
    )
    own_dk, own_dv = (
        lax.psum_scatter(
            long_dk.reshape(long_count, full_len, model_width).astype(jnp.bfloat16),
            "seq",
            scatter_dimension=1,
            tiled=True,
        ).astype(jnp.float32),
        lax.psum_scatter(
            long_dv.reshape(long_count, full_len, model_width).astype(jnp.bfloat16),
            "seq",
            scatter_dimension=1,
            tiled=True,
        ).astype(jnp.float32),
    )
    grad_queries = jnp.concatenate(
        [short_dq.reshape(short_rows, model_width), long_dq.reshape(long_rows, model_width)], axis=0
    ).astype(jnp.bfloat16)
    grad_keys = jnp.concatenate(
        [short_dk.reshape(short_rows, model_width), own_dk.reshape(long_rows, model_width)], axis=0
    ).astype(jnp.bfloat16)
    grad_values = jnp.concatenate(
        [short_dv.reshape(short_rows, model_width), own_dv.reshape(long_rows, model_width)], axis=0
    ).astype(jnp.bfloat16)
    grad_joined = jnp.concatenate([grad_queries, grad_keys, grad_values], axis=1)
    grad_qkv = outer_sum(inputs, grad_joined)
    grad_qv = jnp.stack(
        [
            jnp.sum(grad_queries.astype(jnp.float32), axis=0),
            jnp.sum(grad_values.astype(jnp.float32), axis=0),
        ],
        axis=1,
    )
    grad_inputs = grad_first_in + times_transposed(grad_joined, qkv_matrix)
    grad_out_vec = jnp.stack([grad_bias_one, grad_bias_two], axis=1)
    grad_gains = jnp.stack([grad_gain_one, grad_gain_two], axis=1)
    grad_shifts = jnp.stack([grad_shift_one, grad_shift_two], axis=1)
    shard_grads = (
        lax.psum_scatter(grad_qkv, ("dp", "seq"), scatter_dimension=0, tiled=True),
        lax.psum_scatter(grad_out, ("dp", "seq"), scatter_dimension=0, tiled=True),
        lax.psum_scatter(grad_up, ("dp", "seq"), scatter_dimension=0, tiled=True),
        lax.psum_scatter(grad_down, ("dp", "seq"), scatter_dimension=0, tiled=True),
        lax.psum_scatter(grad_qv, ("dp", "seq"), scatter_dimension=0, tiled=True),
        lax.psum_scatter(grad_out_vec, ("dp", "seq"), scatter_dimension=0, tiled=True),
        lax.psum_scatter(grad_up_bias, ("dp", "seq"), scatter_dimension=0, tiled=True),
        lax.psum_scatter(grad_gains, ("dp", "seq"), scatter_dimension=0, tiled=True),
        lax.psum_scatter(grad_shifts, ("dp", "seq"), scatter_dimension=0, tiled=True),
    )
    short_out = short_final.astype(jnp.bfloat16)
    long_out = long_final.astype(jnp.bfloat16)
    short_grad_in = grad_inputs[:short_rows].reshape(short_count, short_cap, model_width)
    long_grad_in = grad_inputs[short_rows:].reshape(long_count, long_half, model_width)
    return (
        short_out,
        long_out,
        short_pooled,
        long_pooled,
        short_grad_in,
        long_grad_in,
        shard_grads[0],
        shard_grads[1],
        shard_grads[2],
        shard_grads[3],
        shard_grads[4],
        shard_grads[5],
        shard_grads[6],
        shard_grads[7],
        shard_grads[8],
    )


def fast_shards(
    short_tokens, long_tokens, short_len, long_len, short_pool, long_pool, short_cot, long_cot,
    short_pool_cot, long_pool_cot, w_qkv, w_out, w_up, w_down, qv_bias, out_bias, up_bias,
    norm_gain, norm_shift,
):
    groups = lax.axis_size("dp") // 4
    width = w_out.shape[1]
    count, cap, _ = short_tokens.shape
    short_rows = count * cap
    lengths = (short_len, long_len)
    parameters = (
        w_qkv, w_out, w_up, w_down, qv_bias.T, out_bias.T, norm_gain.T, norm_shift.T, up_bias[None, :],
    )
    (down, *kept, vectors, share) = forward(
        lengths,
        parameters,
        (short_pool, long_pool),
        short_tokens.reshape(short_rows, width),
        long_tokens,
        groups,
    )
    arrays = backward(
        lengths,
        vectors,
        share,
        (short_pool_cot, long_pool_cot),
        (short_cot.reshape(short_rows, width), long_cot),
        (down.reshape(4, width, width), *kept),
        groups,
    )
    (
        short_out, long_out, short_pooled, long_pooled, short_grad, long_grad,
        grad_qkv, grad_out, grad_up, grad_down, qv, out, ups, gain, shift,
    ) = results(arrays)
    return (
        short_out.reshape(short_tokens.shape), long_out, short_pooled, long_pooled,
        short_grad.reshape(short_tokens.shape), long_grad, grad_qkv, grad_out, grad_up, grad_down,
        qv.T, out.T, ups[0], gain.T, shift.T,
    )


def solution(mesh):
    short_spec, long_spec, spread = P(("dp", "seq"), None, None), P("dp", "seq", None), P(("dp", "seq"), None)
    vector, parameters = P(("dp", "seq")), [P(("dp", "seq"), None)] * 6
    in_specs = (
        short_spec, long_spec, vector, P("dp"), spread, P("dp", "seq"), short_spec, long_spec,
        spread, P("dp", None), *parameters, vector, spread, spread,
    )
    out_specs = (
        short_spec, long_spec, spread, P("dp", None), short_spec, long_spec, *parameters, vector,
        spread, spread,
    )
    dp, seq = mesh.shape["dp"], mesh.shape["seq"]

    def run(*arrays):
        width = arrays[11].shape[1]
        passages = arrays[1].shape[0] // dp
        regular = dp == 16 and seq == 2 and passages == 2 and width == 24 * dp * seq
        body = fast_shards if regular else general_shards
        return jax.shard_map(body, mesh=mesh, in_specs=in_specs, out_specs=out_specs, check_vma=False)(*arrays)

    return run
```

profile of v0, /device:TPU:0, one launch (start us, length us, event | category | flops | bytes accessed | tf_op | source)
XLA Modules:
  0.0 188.8 jit_solution(4770192063093088463)
XLA Ops:
  0.7 83.8 %forward.1 = (bf16[4,8,96,768]{3,2,1,0:T(8,128)(2,1)}, bf16[4,768,768]{2,1,0:T(8,128)(2,1)}, bf16[4,768,768]{2,1,0:T(8,128)(2,1)}, bf16[1024,768]{1,0:T(8,128)(2...) custom-call(s32[4]{0:T(128)} %short_len.3, ...), custom_call_target="tpu_custom_call" | custom-call | tf_op jit(solution)/shard_map/forward/pallas_call | solution.py:632
  84.5 98.2 %backward.1 = (bf16[512,768]{1,0:T(8,128)(2,1)}, bf16[2,256,768]{2,1,0:T(8,128)(2,1)}, f32[512,768]{1,0:T(8,128)}, f32[2,256,768]{2,1,0:T(8,128)}, f32[4,768]{1,...) custom-call(s32[4]{0:T(128)} %short_len.3, ...), custom_call_target="tpu_custom_call" | custom-call | tf_op jit(solution)/shard_map/backward/pallas_call | solution.py:1136
  182.6 6.0 %results.1 = (bf16[512,768]{1,0:T(8,128)(2,1)}, bf16[2,256,768]{2,1,0:T(8,128)(2,1)}, f32[4,768]{1,0:T(4,128)}, f32[2,768]{1,0:T(2,128)}, f32[512,768]{1,0:T(8,1...) custom-call(bf16[512,768]{1,0:T(8,128)(2,1)} %get-tuple-element.74.i, ...), custom_call_target="tpu_custom_call" | custom-call | tf_op jit(solution)/shard_map/results/pallas_call | solution.py:1184
where the time goes:
time: 189 us
  Pallas kernels  188 us (99%)
    pallas_call x1, Pallas kernels, backward(): pl.pallas_call(backward_kernel, name='backward', out_shape=outs, in_specs...  98.2 us
    pallas_call x1, Pallas kernels, forward(): pl.pallas_call(forward_kernel, name='forward', out_shape=outs, in_specs=[...  83.8 us
    pallas_call x1, Pallas kernels, results(): pl.pallas_call(results_kernel, name='results', out_shape=outs + (pair, pa...  5.97 us

commit v1 on v0

--- a/solution.py
+++ b/solution.py
@@ -411,22 +411,22 @@
         for member in (qv_bias, out_bias, gains, shifts)
         for i in range(2)
     ]
-    ups = put_at(up_bias[...].astype(jnp.float32), lax.rem(device, 8) * (4 * size), width)
-    ups = jnp.where(lax.broadcasted_iota(jnp.int32, (8, 1), 0) == lax.div(device, 8), ups, 0.0)
     z, slot = place.z, place.slot()
     whole0[z, slot] = jnp.concatenate(blocks(w_qkv) + pairs, axis=0).astype(jnp.bfloat16)
-    whole1[z, slot] = jnp.concatenate(blocks(w_out) + [ups], axis=0).astype(jnp.bfloat16)
-    whole2[z, slot] = jnp.concatenate(blocks(w_up), axis=0).astype(jnp.bfloat16)
 
     place.greet_wait()
     wires = Wires(send, recv)
     net = Gather(wires, place, (whole0, whole1, whole2, out_down), w_down)
     net.start(0)
+    net.start_plane(0)
+    ups = put_at(up_bias[...].astype(jnp.float32), lax.rem(device, 8) * (4 * size), width)
+    ups = jnp.where(lax.broadcasted_iota(jnp.int32, (8, 1), 0) == lax.div(device, 8), ups, 0.0)
+    whole1[z, slot] = jnp.concatenate(blocks(w_out) + [ups], axis=0).astype(jnp.bfloat16)
     net.start(1)
+    net.start_plane(1)
+    whole2[z, slot] = jnp.concatenate(blocks(w_up), axis=0).astype(jnp.bfloat16)
+    net.start(2)
     net.start_plane(2)
-    net.start(2)
-    net.start_plane(1)
-    net.start_plane(0)
     pooled = wires.put(long_pool, far_pool, place.at_x())
     net.relay_z(0)
     net.relay_plane(0)
@@ -1147,17 +1147,23 @@
 
 
 def results_kernel(
-    in_0, in_1, in_2, in_3, in_4, in_5, in_6, in_7, in_8, in_9, grad_vectors, grad_ups,
+    in_0, in_1, in_2, in_3, in_4, in_5, in_6, in_7, in_8, in_9, in_10, in_11,
     out_0, out_1, out_2, out_3, out_4, out_5, out_6, out_7, out_8, out_9, pair_0, pair_1, ups, pair_2, pair_3,
     *more,
 ):
     *held, come, leave = more
-    sources = (in_0, in_1, in_2, in_3, in_4, in_5, in_6, in_7, in_8, in_9)
+    grad_vectors, grad_ups = held[10:]
+    sources = (in_0, in_1, in_2, in_3, in_4, in_5, in_6, in_7, in_8, in_9, in_10, in_11)
     places = (out_0, out_1, out_4, out_5, out_2, out_3, out_6, out_7, out_8, out_9)
-    ins = [pltpu.make_async_copy(sources[i], held[i], come.at[i]) for i in range(10)]
+    ins = [pltpu.make_async_copy(sources[i], held[i], come.at[i]) for i in range(12)]
     outs = [pltpu.make_async_copy(held[i], places[i], leave.at[i]) for i in range(10)]
     for copy in ins:
         copy.start()
+    for i in range(10):
+        ins[i].wait()
+        outs[i].start()
+    ins[10].wait()
+    ins[11].wait()
     device = lax.axis_index("dp") * 2 + lax.axis_index("seq")
     size, width = in_7.shape
     rows = pltpu.roll(grad_vectors[...], lax.rem(width - device * size, width), 1)
@@ -1167,9 +1173,6 @@
     row = grad_ups[pl.ds(lax.div(device, 8), 1), :]
     row = pltpu.roll(jnp.broadcast_to(row, (8, width)), lax.rem(width - start, width), 1)
     ups[...] = row[0:1, 0 : 4 * size]
-    for i in range(10):
-        ins[i].wait()
-        outs[i].start()
     for copy in outs:
         copy.wait()
 
@@ -1185,10 +1188,10 @@
         results_kernel,
         name="results",
         out_shape=outs + (pair, pair, shape((1, 4 * size), jnp.float32), pair, pair),
-        in_specs=[anywhere] * 10 + [near] * 2,
+        in_specs=[anywhere] * 12,
         out_specs=[anywhere] * 10 + [near] * 5,
-        scratch_shapes=[pltpu.VMEM(array.shape, array.dtype) for array in arrays[:10]]
-        + [pltpu.SemaphoreType.DMA((10,)), pltpu.SemaphoreType.DMA((10,))],
+        scratch_shapes=[pltpu.VMEM(array.shape, array.dtype) for array in arrays]
+        + [pltpu.SemaphoreType.DMA((12,)), pltpu.SemaphoreType.DMA((10,))],
         compiler_params=pltpu.CompilerParams(vmem_limit_bytes=56 * 1024 * 1024),
     )(*arrays)
 

time: 189 us -> 188 us (level)
  no operation moved by 1% of the time
where the time goes in v1:
time: 188 us
  Pallas kernels  187 us (99%)
    pallas_call x1, Pallas kernels, backward(): pl.pallas_call(backward_kernel, name='backward', out_shape=outs, in_specs...  98.1 us
    pallas_call x1, Pallas kernels, forward(): pl.pallas_call(forward_kernel, name='forward', out_shape=outs, in_specs=[...  83.8 us
    pallas_call x1, Pallas kernels, results(): pl.pallas_call(results_kernel, name='results', out_shape=outs + (pair, pa...  5.23 us

profile of v1, /device:TPU:0, one launch (start us, length us, event | category | flops | bytes accessed | tf_op | source)
XLA Modules:
  0.0 188.0 jit_solution(382093393999579438)
XLA Ops:
  0.7 83.8 %forward.1 = (bf16[4,8,96,768]{3,2,1,0:T(8,128)(2,1)}, bf16[4,768,768]{2,1,0:T(8,128)(2,1)}, bf16[4,768,768]{2,1,0:T(8,128)(2,1)}, bf16[1024,768]{1,0:T(8,128)(2...) custom-call(s32[4]{0:T(128)} %short_len.3, ...), custom_call_target="tpu_custom_call" | custom-call | tf_op jit(solution)/shard_map/forward/pallas_call | solution.py:632
  84.5 98.1 %backward.1 = (bf16[512,768]{1,0:T(8,128)(2,1)}, bf16[2,256,768]{2,1,0:T(8,128)(2,1)}, f32[512,768]{1,0:T(8,128)}, f32[2,256,768]{2,1,0:T(8,128)}, f32[4,768]{1,...) custom-call(s32[4]{0:T(128)} %short_len.3, ...), custom_call_target="tpu_custom_call" | custom-call | tf_op jit(solution)/shard_map/backward/pallas_call | solution.py:1136
  182.6 5.2 %results.1 = (bf16[512,768]{1,0:T(8,128)(2,1)}, bf16[2,256,768]{2,1,0:T(8,128)(2,1)}, f32[4,768]{1,0:T(4,128)}, f32[2,768]{1,0:T(2,128)}, f32[512,768]{1,0:T(8,1...) custom-call(bf16[512,768]{1,0:T(8,128)(2,1)} %get-tuple-element.74.i, ...), custom_call_target="tpu_custom_call" | custom-call | tf_op jit(solution)/shard_map/results/pallas_call | solution.py:1187
